TPU v7x, 128 devices: a whole 4x4x4 slice. The times are simulated.
128 devices in a mesh: section: 4 (over x_hi, core), field: 4 (over y), dp: 8 (over x_lo, z).
Axes of the slice: x: 4 (x_hi: 2, x_lo: 2; x = x_hi * 2 + x_lo), y: 4, z: 4, core: 2. Of those that a mesh axis runs over, the one named last changes fastest.
Arguments:
- patches: bfloat16 [4, 1024, 8, 512], P(None, 'dp', 'field'), may hold values from -6 to 6
- field_mask: int32 [4, 1024, 8], P(None, 'dp', 'field'), may hold values 0 or 1
- order: int32 [4], replicated, may hold values from 0 to 3, each once
- embed_weight: bfloat16 [8, 512, 4096], P('field'), may hold values from -0.09375 to 0.09375
- embed_bias: bfloat16 [8, 4096], P('field'), may hold values from -3 to 3
- norm_gain: float32 [4, 4096], P('section'), may hold values from 0.1 to 1.9
- w_up: bfloat16 [4, 4096, 5632], P('section', 'dp', 'field'), may hold values from -0.09375 to 0.09375
- w_down: bfloat16 [4, 5632, 4096], P('section', 'field', 'dp'), may hold values from -0.109375 to 0.109375
Outputs:
- hidden_out: bfloat16 [4, 1024, 4096], P('section', 'dp', 'field')
Inputs may be any that keep to these rules, and one draw needn't show every extreme that they name: `order`: each micro-batch appears once.
All inputs are finite; a program needn't handle non-finite values. No bound on the sum of `field_mask` on one device may be relied on, other than what follows from the above.
Results may differ from a plain program's by a relative error of at most 0.03.
Values may be sent and summed in bfloat16 or wider, within the bound.
No kernel may reach another device: no remote copies, remote signals or barrier semaphores. Data moves between devices by JAX's collectives and lax.ppermute only.
A program may use at most 128 MiB of HBM per device.

v0:
```python
import jax
import jax.numpy as jnp
from jax import lax
from jax.sharding import PartitionSpec as P


def from_behind(block, axis, distance):
    devices = range(lax.axis_size(axis))
    route = [(i - distance, i) for i in devices if i - distance in devices]
    return lax.ppermute(block, axis, route)


def embed_term(patches, field_mask, order, embed_weight, embed_bias, position):
    chosen = order[position]
    piece = lax.dynamic_index_in_dim(patches, chosen, 0, keepdims=False)
    present = lax.dynamic_index_in_dim(field_mask, chosen, 0, keepdims=False)
    masked = piece * present.astype(jnp.bfloat16)[:, :, None]
    term = jnp.einsum("tfp,fpd->td", masked, embed_weight, preferred_element_type=jnp.float32)
    term = term + jnp.dot(
        present.astype(jnp.bfloat16), embed_bias, preferred_element_type=jnp.float32
    )
    return lax.optimization_barrier(term.astype(jnp.bfloat16)).astype(jnp.float32)


def reduce_embed(term):
    return lax.psum_scatter(term.astype(jnp.bfloat16), "field", scatter_dimension=1, tiled=True)


def per_device(patches, field_mask, order, embed_weight, embed_bias, norm_gain, w_up, w_down):
    section = lax.axis_index("section")
    n_section = lax.axis_size("section")
    micro = patches.shape[0]
    tokens = patches.shape[1]
    width = embed_weight.shape[2]
    narrow = width // lax.axis_size("field")
    up_full, down_full = (
        lax.all_gather(w_up[0], "dp", axis=0, tiled=True),
        lax.all_gather(w_down[0], "dp", axis=1, tiled=True),
    )
    gain = norm_gain[0][None, :]

    def local_layer(full):
        values = full.astype(jnp.float32)
        scale = lax.rsqrt(jnp.mean(values * values, axis=-1, keepdims=True) + 1e-05)
        normed = (values * scale * gain).astype(jnp.bfloat16)
        upward = jnp.dot(normed, up_full, preferred_element_type=jnp.float32)
        active = jax.nn.gelu(upward, approximate=True).astype(jnp.bfloat16)
        part = jnp.dot(active, down_full, preferred_element_type=jnp.float32)
        return lax.optimization_barrier(part.astype(jnp.bfloat16)).astype(jnp.float32)

    def skipped(full):
        return jnp.zeros((tokens, width), jnp.float32)

    def first_term(position):
        return lambda operand: embed_term(
            patches, field_mask, order, embed_weight, embed_bias, position
        )

    def empty_term(operand):
        return jnp.zeros((tokens, width), jnp.float32)

    state = jnp.zeros((tokens, narrow), jnp.bfloat16)
    results = []
    ticks = micro + n_section - 1
    for tick in range(ticks):
        if tick < micro:
            term = lax.cond(section == 0, first_term(tick), empty_term, 0)
            entering = reduce_embed(term)
            state = jnp.where(section == 0, entering, state)
        step = tick - section
        valid = jnp.logical_and(step >= 0, step < micro)
        run_full = lax.all_gather(state, "field", axis=1, tiled=True)
        run_part = lax.cond(valid, local_layer, skipped, run_full)
        summed = lax.psum_scatter(
            run_part.astype(jnp.bfloat16), "field", scatter_dimension=1, tiled=True
        ).astype(jnp.float32)
        output = (state.astype(jnp.float32) + summed).astype(jnp.bfloat16)
        finish = tick - (n_section - 1)
        if finish >= 0:
            results.append(jnp.where(section == n_section - 1, output, jnp.zeros_like(output)))
        if tick + 1 < ticks:
            state = from_behind(output, "section", 1)
    finished_all = jnp.stack(results)
    kept = lax.psum_scatter(
        finished_all.astype(jnp.float32).astype(jnp.bfloat16),
        "section",
        scatter_dimension=0,
        tiled=True,
    )
    return kept


def solution(mesh):
    in_specs = (
        P(None, "dp", "field", None),
        P(None, "dp", "field"),
        P(),
        P("field", None, None),
        P("field", None),
        P("section", None),
        P("section", "dp", "field"),
        P("section", "field", "dp"),
    )
    out_specs = P("section", "dp", "field")
    return jax.shard_map(
        per_device, mesh=mesh, in_specs=in_specs, out_specs=out_specs, check_vma=False
    )
```

profile of v0, /device:TPU:24, one launch (start us, length us, event | category | flops | bytes accessed | tf_op | source)
XLA Modules:
  0.0 869.8 jit_solution(1163121636016504278)
XLA Ops:
  14.5 22.2 %reduce-scatter.19.cloned.1.call-done = bf16[128,1024]{1,0:T(8,128)(2,1)} async-done(((bf16[128,4096]{1,0:T(8,128)(2,1)}), bf16[128,1024]{1,0:T(8,128)(2,1)}) %reduce-scatter.19.cloned.1.call-update) | async-done | bytes 262160 | tf_op jit(solution)/shard_map/reduce_scatter | solution.py:26
  39.7 23.5 %all-gather.12.cloned.1.call-done = bf16[128,4096]{1,0:T(8,128)(2,1)} async-done(((bf16[128,1024]{1,0:T(8,128)(2,1)}), bf16[128,4096]{1,0:T(8,128)(2,1)}) %all-gather.12.cloned.1.call-update) | async-done | bytes 1048592 | tf_op jit(solution)/shard_map/all_gather | solution.py:72
  63.2 124.7 %all-gather.26.cloned.1.call-done = bf16[1,4096,1408]{2,1,0:T(8,128)(2,1)} async-done(((bf16[1,512,1408]{2,1,0:T(8,128)(2,1)}), bf16[1,4096,1408]{2,1,0:T(8,128)(2,1)}) %all-gather.26.cloned.1.call-update) | async-done | bytes 11534352 | tf_op jit(solution)/shard_map/all_gather | solution.py:37
  187.9 121.9 %all-gather.28.cloned.1.call-done = bf16[1,1408,4096]{2,1,0:T(8,128)(2,1)} async-done(((bf16[1,1408,512]{2,1,0:T(8,128)(2,1)}), bf16[1,1408,4096]{2,1,0:T(8,128)(2,1)}) %all-gather.28.cloned.1.call-update) | async-done | bytes 11534352 | tf_op jit(solution)/shard_map/all_gather | solution.py:38
  309.8 13.1 %conditional.15 = (bf16[128,4096]{1,0:T(8,128)(2,1)S(1)}) conditional(s32[]{:T(128)} %convert_element_type.304, () %tuple.76, (bf16[128,4096]{1,0:T(8,128)(2,1)}, f32[1,4096]{1,0:T(1,128)S(1)}, bf16[4096,1408]{1,0:T(8,128)(2,1)}, bf16[1408,4096]{1,0:T(8,128)(2,1)}) %tuple.175), branch_computations={%region_12.13_spmd, %region_13.15_spmd} | conditional | flops 2958606336 | bytes 26232840 | solution.py:73
  345.2 23.1 %reduce-scatter.17.cloned.1.call-done = bf16[128,1024]{1,0:T(8,128)(2,1)} async-done(((bf16[128,4096]{1,0:T(8,128)(2,1)}), bf16[128,1024]{1,0:T(8,128)(2,1)}) %reduce-scatter.17.cloned.1.call-update) | async-done | bytes 262160 | tf_op jit(solution)/shard_map/reduce_scatter | solution.py:26
  370.1 24.8 %all-gather.14.cloned.1.call-done = bf16[128,4096]{1,0:T(8,128)(2,1)} async-done(((bf16[128,1024]{1,0:T(8,128)(2,1)}), bf16[128,4096]{1,0:T(8,128)(2,1)}) %all-gather.14.cloned.1.call-update) | async-done | bytes 1048592 | tf_op jit(solution)/shard_map/all_gather | solution.py:72
  394.9 13.2 %conditional.16 = (bf16[128,4096]{1,0:T(8,128)(2,1)S(1)}) conditional(s32[]{:T(128)} %convert_element_type.309, () %tuple.78, (bf16[128,4096]{1,0:T(8,128)(2,1)}, f32[1,4096]{1,0:T(1,128)S(1)}, bf16[4096,1408]{1,0:T(8,128)(2,1)}, bf16[1408,4096]{1,0:T(8,128)(2,1)}) %tuple.176), branch_computations={%region_16.17_spmd, %region_17.19_spmd} | conditional | flops 2958606336 | bytes 26232840 | solution.py:73
  418.1 12.5 %reduce-scatter.23.cloned.1.call-done = bf16[128,1024]{1,0:T(8,128)(2,1)} async-done(((bf16[128,4096]{1,0:T(8,128)(2,1)}), bf16[128,1024]{1,0:T(8,128)(2,1)}) %reduce-scatter.23.cloned.1.call-update) | async-done | bytes 262160 | tf_op jit(solution)/shard_map/reduce_scatter | solution.py:74
  432.9 23.3 %reduce-scatter.15.cloned.1.call-done = bf16[128,1024]{1,0:T(8,128)(2,1)} async-done(((bf16[128,4096]{1,0:T(8,128)(2,1)}), bf16[128,1024]{1,0:T(8,128)(2,1)}) %reduce-scatter.15.cloned.1.call-update) | async-done | bytes 262160 | tf_op jit(solution)/shard_map/reduce_scatter | solution.py:26
  458.0 24.6 %all-gather.16.cloned.1.call-done = bf16[128,4096]{1,0:T(8,128)(2,1)} async-done(((bf16[128,1024]{1,0:T(8,128)(2,1)}), bf16[128,4096]{1,0:T(8,128)(2,1)}) %all-gather.16.cloned.1.call-update) | async-done | bytes 1048592 | tf_op jit(solution)/shard_map/all_gather | solution.py:72
  482.6 13.1 %conditional.17 = (bf16[128,4096]{1,0:T(8,128)(2,1)S(1)}) conditional(s32[]{:T(128)} %convert_element_type.314, () %tuple.80, (bf16[128,4096]{1,0:T(8,128)(2,1)}, f32[1,4096]{1,0:T(1,128)S(1)}, bf16[4096,1408]{1,0:T(8,128)(2,1)}, bf16[1408,4096]{1,0:T(8,128)(2,1)}) %tuple.177), branch_computations={%region_20.21_spmd, %region_21.23_spmd} | conditional | flops 2958606336 | bytes 26232840 | solution.py:73
  505.6 14.0 %reduce-scatter.25.cloned.1.call-done = bf16[128,1024]{1,0:T(8,128)(2,1)} async-done(((bf16[128,4096]{1,0:T(8,128)(2,1)}), bf16[128,1024]{1,0:T(8,128)(2,1)}) %reduce-scatter.25.cloned.1.call-update) | async-done | bytes 262160 | tf_op jit(solution)/shard_map/reduce_scatter | solution.py:74
  521.9 23.2 %reduce-scatter.13.cloned.1.call-done = bf16[128,1024]{1,0:T(8,128)(2,1)} async-done(((bf16[128,4096]{1,0:T(8,128)(2,1)}), bf16[128,1024]{1,0:T(8,128)(2,1)}) %reduce-scatter.13.cloned.1.call-update) | async-done | bytes 262160 | tf_op jit(solution)/shard_map/reduce_scatter | solution.py:26
  547.1 24.5 %all-gather.18.cloned.1.call-done = bf16[128,4096]{1,0:T(8,128)(2,1)} async-done(((bf16[128,1024]{1,0:T(8,128)(2,1)}), bf16[128,4096]{1,0:T(8,128)(2,1)}) %all-gather.18.cloned.1.call-update) | async-done | bytes 1048592 | tf_op jit(solution)/shard_map/all_gather | solution.py:72
  571.6 13.1 %conditional.18 = (bf16[128,4096]{1,0:T(8,128)(2,1)S(1)}) conditional(s32[]{:T(128)} %convert_element_type.319, () %tuple.82, (bf16[128,4096]{1,0:T(8,128)(2,1)}, f32[1,4096]{1,0:T(1,128)S(1)}, bf16[4096,1408]{1,0:T(8,128)(2,1)}, bf16[1408,4096]{1,0:T(8,128)(2,1)}) %tuple.178), branch_computations={%region_24.25_spmd, %region_25.27_spmd} | conditional | flops 2958606336 | bytes 26232840 | solution.py:73
  585.7 22.9 %reduce-scatter.27.cloned.1.call-done = bf16[128,1024]{1,0:T(8,128)(2,1)} async-done(((bf16[128,4096]{1,0:T(8,128)(2,1)}), bf16[128,1024]{1,0:T(8,128)(2,1)}) %reduce-scatter.27.cloned.1.call-update) | async-done | bytes 262160 | tf_op jit(solution)/shard_map/reduce_scatter | solution.py:74
  612.9 31.6 %all-gather.20.cloned.1.call-done = bf16[128,4096]{1,0:T(8,128)(2,1)} async-done(((bf16[128,1024]{1,0:T(8,128)(2,1)}), bf16[128,4096]{1,0:T(8,128)(2,1)}) %all-gather.20.cloned.1.call-update) | async-done | bytes 1048592 | tf_op jit(solution)/shard_map/all_gather | solution.py:72
  645.7 35.9 %reduce-scatter.29.cloned.1.call-done = bf16[128,1024]{1,0:T(8,128)(2,1)} async-done(((bf16[128,4096]{1,0:T(8,128)(2,1)}), bf16[128,1024]{1,0:T(8,128)(2,1)}) %reduce-scatter.29.cloned.1.call-update) | async-done | bytes 262160 | tf_op jit(solution)/shard_map/reduce_scatter | solution.py:74
  685.8 31.6 %all-gather.22.cloned.1.call-done = bf16[128,4096]{1,0:T(8,128)(2,1)} async-done(((bf16[128,1024]{1,0:T(8,128)(2,1)}), bf16[128,4096]{1,0:T(8,128)(2,1)}) %all-gather.22.cloned.1.call-update) | async-done | bytes 1048592 | tf_op jit(solution)/shard_map/all_gather | solution.py:72
  718.8 35.6 %reduce-scatter.31.cloned.1.call-done = bf16[128,1024]{1,0:T(8,128)(2,1)} async-done(((bf16[128,4096]{1,0:T(8,128)(2,1)}), bf16[128,1024]{1,0:T(8,128)(2,1)}) %reduce-scatter.31.cloned.1.call-update) | async-done | bytes 262160 | tf_op jit(solution)/shard_map/reduce_scatter | solution.py:74
  758.7 31.6 %all-gather.24.cloned.1.call-done = bf16[128,4096]{1,0:T(8,128)(2,1)} async-done(((bf16[128,1024]{1,0:T(8,128)(2,1)}), bf16[128,4096]{1,0:T(8,128)(2,1)}) %all-gather.24.cloned.1.call-update) | async-done | bytes 1048592 | tf_op jit(solution)/shard_map/all_gather | solution.py:72
  791.6 34.6 %reduce-scatter.33.cloned.1.call-done = bf16[128,1024]{1,0:T(8,128)(2,1)} async-done(((bf16[128,4096]{1,0:T(8,128)(2,1)}), bf16[128,1024]{1,0:T(8,128)(2,1)}) %reduce-scatter.33.cloned.1.call-update) | async-done | bytes 262160 | tf_op jit(solution)/shard_map/reduce_scatter | solution.py:74
  828.4 34.2 %reduce-scatter.35.cloned.1.call-done = bf16[1,128,1024]{2,1,0:T(8,128)(2,1)} async-done(((bf16[4,128,1024]{2,1,0:T(8,128)(2,1)}), bf16[1,128,1024]{2,1,0:T(8,128)(2,1)}) %reduce-scatter.35.cloned.1.call-update) | async-done | bytes 262160 | tf_op jit(solution)/shard_map/reduce_scatter | solution.py:84
  (155 shorter events, 157.9 us)
Async XLA Ops:
  6.5 30.1 %reduce-scatter.19.cloned.1.call-start = ((), (), s32[]{:S(2)}) async-start(), calls=%async_computation.15 | async-start | bytes 1310720 | tf_op jit(solution)/shard_map/reduce_scatter | solution.py:26
  14.4 48.8 %all-gather.12.cloned.1.call-start = ((), (), s32[]{:S(2)}) async-start(), calls=%async_computation.16 | async-start | bytes 1310720 | tf_op jit(solution)/shard_map/all_gather | solution.py:72
  38.4 149.5 %all-gather.26.cloned.1.call-start = ((), (), s32[]{:S(2)}) async-start(), calls=%async_computation.31 | async-start | bytes 12976128 | tf_op jit(solution)/shard_map/all_gather | solution.py:37
  39.1 270.6 %all-gather.28.cloned.1.call-start = ((), (), s32[]{:S(2)}) async-start(), calls=%async_computation.32 | async-start | bytes 12976128 | tf_op jit(solution)/shard_map/all_gather | solution.py:38
  39.7 303.1 %reduce-scatter.21.cloned.1.call-start = ((), (), s32[]{:S(2)}) async-start(), calls=%async_computation.17 | async-start | bytes 1310720 | tf_op jit(solution)/shard_map/reduce_scatter | solution.py:74
  323.9 44.4 %reduce-scatter.17.cloned.1.call-start = ((), (), s32[]{:S(2)}) async-start(), calls=%async_computation.14 | async-start | bytes 1310720 | tf_op jit(solution)/shard_map/reduce_scatter | solution.py:26
  332.7 62.1 %all-gather.14.cloned.1.call-start = ((), (), s32[]{:S(2)}) async-start(), calls=%async_computation.18 | async-start | bytes 1310720 | tf_op jit(solution)/shard_map/all_gather | solution.py:72
  343.8 24.5 %collective-permute-start = (bf16[128,1024]{1,0:T(8,128)(2,1)S(1)}, bf16[128,1024]{1,0:T(8,128)(2,1)S(1)}, u32[]{:S(2)}, u32[]{:S(2)}) collective-permute-start(bf16[128,1024]{1,0:T(8,128)(2,1)S(1)} %add_convert_fusion.6), channel_id=1, source_target_pairs={{0,32},{32,64},{64,96},{1,33},{33,65},{65,97},{2,34},{34,66},{66,9... | collective-permute-start | bytes 786440 | tf_op jit(solution)/shard_map/ppermute | solution.py:10
  370.0 60.5 %reduce-scatter.23.cloned.1.call-start = ((), (), s32[]{:S(2)}) async-start(), calls=%async_computation.19 | async-start | bytes 1310720 | tf_op jit(solution)/shard_map/reduce_scatter | solution.py:74
  409.1 47.1 %reduce-scatter.15.cloned.1.call-start = ((), (), s32[]{:S(2)}) async-start(), calls=%async_computation.13 | async-start | bytes 1310720 | tf_op jit(solution)/shard_map/reduce_scatter | solution.py:26
  418.0 64.5 %all-gather.16.cloned.1.call-start = ((), (), s32[]{:S(2)}) async-start(), calls=%async_computation.20 | async-start | bytes 1310720 | tf_op jit(solution)/shard_map/all_gather | solution.py:72
  431.6 24.6 %collective-permute-start.1 = (bf16[128,1024]{1,0:T(8,128)(2,1)S(1)}, bf16[128,1024]{1,0:T(8,128)(2,1)S(1)}, u32[]{:S(2)}, u32[]{:S(2)}) collective-permute-start(bf16[128,1024]{1,0:T(8,128)(2,1)S(1)} %add_convert_fusion.5), channel_id=1, source_target_pairs={{0,32},{32,64},{64,96},{1,33},{33,65},{65,97},{2,34},{34,66},{66,9... | collective-permute-start | bytes 786440 | tf_op jit(solution)/shard_map/ppermute | solution.py:10
  457.9 61.7 %reduce-scatter.25.cloned.1.call-start = ((), (), s32[]{:S(2)}) async-start(), calls=%async_computation.21 | async-start | bytes 1310720 | tf_op jit(solution)/shard_map/reduce_scatter | solution.py:74
  496.6 48.5 %reduce-scatter.13.cloned.1.call-start = ((), (), s32[]{:S(2)}) async-start(), calls=%async_computation.12 | async-start | bytes 1310720 | tf_op jit(solution)/shard_map/reduce_scatter | solution.py:26
  505.5 66.1 %all-gather.18.cloned.1.call-start = ((), (), s32[]{:S(2)}) async-start(), calls=%async_computation.22 | async-start | bytes 1310720 | tf_op jit(solution)/shard_map/all_gather | solution.py:72
  520.6 24.5 %collective-permute-start.2 = (bf16[128,1024]{1,0:T(8,128)(2,1)S(1)}, bf16[128,1024]{1,0:T(8,128)(2,1)S(1)}, u32[]{:S(2)}, u32[]{:S(2)}) collective-permute-start(bf16[128,1024]{1,0:T(8,128)(2,1)S(1)} %add_convert_fusion.4), channel_id=1, source_target_pairs={{0,32},{32,64},{64,96},{1,33},{33,65},{65,97},{2,34},{34,66},{66,9... | collective-permute-start | bytes 786440 | tf_op jit(solution)/shard_map/ppermute | solution.py:10
  546.8 61.8 %reduce-scatter.27.cloned.1.call-start = ((), (), s32[]{:S(2)}) async-start(), calls=%async_computation.23 | async-start | bytes 1310720 | tf_op jit(solution)/shard_map/reduce_scatter | solution.py:74
  585.7 58.8 %all-gather.20.cloned.1.call-start = ((), (), s32[]{:S(2)}) async-start(), calls=%async_computation.24 | async-start | bytes 1310720 | tf_op jit(solution)/shard_map/all_gather | solution.py:72
  612.9 68.7 %reduce-scatter.29.cloned.1.call-start = ((), (), s32[]{:S(2)}) async-start(), calls=%async_computation.25 | async-start | bytes 1310720 | tf_op jit(solution)/shard_map/reduce_scatter | solution.py:74
  645.6 71.8 %all-gather.22.cloned.1.call-start = ((), (), s32[]{:S(2)}) async-start(), calls=%async_computation.26 | async-start | bytes 1310720 | tf_op jit(solution)/shard_map/all_gather | solution.py:72
  685.8 68.7 %reduce-scatter.31.cloned.1.call-start = ((), (), s32[]{:S(2)}) async-start(), calls=%async_computation.27 | async-start | bytes 1310720 | tf_op jit(solution)/shard_map/reduce_scatter | solution.py:74
  718.5 71.9 %all-gather.24.cloned.1.call-start = ((), (), s32[]{:S(2)}) async-start(), calls=%async_computation.28 | async-start | bytes 1310720 | tf_op jit(solution)/shard_map/all_gather | solution.py:72
  758.7 67.5 %reduce-scatter.33.cloned.1.call-start = ((), (), s32[]{:S(2)}) async-start(), calls=%async_computation.29 | async-start | bytes 1310720 | tf_op jit(solution)/shard_map/reduce_scatter | solution.py:74
  791.5 71.0 %reduce-scatter.35.cloned.1.call-start = ((), (), s32[]{:S(2)}) async-start(), calls=%async_computation.30 | async-start | bytes 1310720 | tf_op jit(solution)/shard_map/reduce_scatter | solution.py:84
  (28 other events, 530.3 us)
Sparse Core Ops, SparseCore 0:
  14.5 22.0 reduce-scatter.18
  38.5 24.6 all-gather.11
  65.0 122.8 all-gather.25
  189.5 120.2 all-gather.27
  324.0 18.7 reduce-scatter.20
  345.1 23.1 reduce-scatter.16
  370.1 24.6 all-gather.13
  409.2 21.2 reduce-scatter.22
  432.9 23.2 reduce-scatter.14
  458.0 24.4 all-gather.15
  496.7 22.7 reduce-scatter.24
  521.8 23.2 reduce-scatter.12
  546.9 24.6 all-gather.17
  585.8 22.7 reduce-scatter.26
  613.0 31.4 all-gather.19
  646.8 34.7 reduce-scatter.28
  685.9 31.4 all-gather.21
  719.8 34.6 reduce-scatter.30
  758.8 31.5 all-gather.23
  792.6 33.4 reduce-scatter.32
  829.0 33.5 reduce-scatter.34
where the time goes:
time: 878 us; the launch traced here: 870 us
  waiting for transfers between devices  735 us (84%)
  matrix products  66.8 us (8%)
  other arithmetic  21.3 us (2%)
  local copies, waits for them, and re-layouts  16.8 us (2%)
  between operations  14.5 us (2%)
  starting transfers between devices  9.12 us (1%)
    all_gather x7, waiting for transfers between devices, per_device(): run_full = lax.all_gather(state, 'field', axis=1, tiled=True)  192 us
    reduce_scatter x7, waiting for transfers between devices, per_device(): lax.psum_scatter(run_part.astype(jnp.bfloat16), 'field', scatter_dimensio...  165 us
    all_gather x1, waiting for transfers between devices, per_device(): lax.all_gather(w_up[0], 'dp', axis=0, tiled=True)  125 us
    all_gather x1, waiting for transfers between devices, per_device(): lax.all_gather(w_down[0], 'dp', axis=1, tiled=True)  122 us
    reduce_scatter x4, waiting for transfers between devices, reduce_embed(): lax.psum_scatter(term.astype(jnp.bfloat16), 'field', scatter_dimension=1,...  91.8 us
    dot_general x4, matrix products, local_layer(): part = jnp.dot(active, down_full, preferred_element_type=jnp.float32)  46.1 us
    reduce_scatter x1, waiting for transfers between devices, per_device(): lax.psum_scatter(finished_all.astype(jnp.float32).astype(jnp.bfloat16), '...  34.2 us
    dot_general x4, matrix products, embed_term(): jnp.einsum('tfp,fpd->td', masked, embed_weight, preferred_element_type=jn...  18.8 us
  transfers between devices with their start and end apart: 27, of which 24 were waited for; matrix products, arithmetic and copies ran while one was open for 2% of the time, Pallas kernels for 0%

commit v1 on v0

v1 whole, which is shorter than its diff:
```python
import jax
import jax.numpy as jnp
from jax import lax
from jax.experimental import pallas as pl
from jax.experimental.pallas import tpu as pltpu
from jax.sharding import Mesh, PartitionSpec as P

AXES = ("xh", "core", "y", "xl", "z")
SIZES = (2, 2, 4, 2, 4)
RING = 4
EPS = 1e-05
VMEM = pl.BlockSpec(memory_space=pltpu.VMEM)
SMEM = pl.BlockSpec(memory_space=pltpu.SMEM)


def call(kernel, out_shape, in_specs, scratch=(), flops=0, nbytes=0):
    return pl.pallas_call(
        kernel,
        out_shape=out_shape,
        in_specs=in_specs,
        out_specs=jax.tree.map(lambda _: VMEM, out_shape),
        scratch_shapes=list(scratch),
        compiler_params=pltpu.CompilerParams(vmem_limit_bytes=40 * 2**20),
        cost_estimate=pl.CostEstimate(flops=flops, bytes_accessed=nbytes, transcendentals=0),
    )


def embed_kernel(place, masked, present, weight, bias, *outs):
    core, y = place[0], place[1]
    half = 256
    piece = masked[...]
    for ahead in range(RING):
        block = lax.rem(y + ahead, RING)
        for xl in range(2):
            for rel in range(2):
                side = core if rel == 0 else 1 - core
                start = (block + RING * xl) * (2 * half) + side * half
                at = pl.ds(pl.multiple_of(start, half), half)
                total = jnp.dot(
                    piece, weight[:, at], preferred_element_type=jnp.float32
                )
                for f in range(2):
                    total += present[:, f : f + 1] * bias[f : f + 1, at].astype(jnp.float32)
                outs[ahead][:, pl.ds(xl * 2 * half + rel * half, half)] = total.astype(
                    jnp.bfloat16
                )


def up_kernel(place, x0, x1, x2, x3, own, other, *rest):
    outs, (held, made) = rest[:RING], rest[RING:]
    y, z = place[1], place[2]
    for behind, block in enumerate((x0, x1, x2, x3)):
        held[lax.rem(y + RING - behind, RING)] = block[...]
    rows = held.shape[0] * held.shape[1]
    hidden = own.shape[2]
    half = own.shape[1]
    x = held[...].reshape(rows, held.shape[2])
    for start in range(0, hidden, 256):
        wide = min(256, hidden - start)
        at = slice(start, start + wide)
        total = jnp.zeros((rows, wide), jnp.float32)
        for xl in range(2):
            for rel, part in enumerate((own, other)):
                k = (xl * 2 + rel) * half
                total += jnp.dot(
                    x[:, k : k + half], part[xl, :, at], preferred_element_type=jnp.float32
                )
        made[:, :, at] = total.astype(jnp.bfloat16).reshape(RING, rows // RING, wide)
    values = x.astype(jnp.float32)
    square = jnp.sum(values * values, axis=1, keepdims=True)
    high = square.astype(jnp.bfloat16).astype(jnp.float32)
    lane = lax.broadcasted_iota(jnp.int32, (rows, 128), 1)
    tail = jnp.where(lane == 0, high, jnp.where(lane == 1, square - high, 0.0))
    made[:, :, hidden:] = tail.astype(jnp.bfloat16).reshape(RING, rows // RING, 128)
    for ahead in range(RING):
        outs[ahead][...] = made[lax.rem(z + ahead, RING)]


def act_kernel(width, h0, h1, h2, h3, out):
    hidden = out.shape[1]
    blocks = (h0, h1, h2, h3)
    square = jnp.zeros((out.shape[0], 1), jnp.float32)
    for block in blocks:
        tail = block[:, hidden:].astype(jnp.float32)
        square += jnp.sum(tail, axis=1, keepdims=True)
    scale = lax.rsqrt(square / width + EPS)
    total = jnp.zeros(out.shape, jnp.float32)
    for block in blocks:
        total += block[:, :hidden].astype(jnp.float32)
    out[...] = jax.nn.gelu(total * scale, approximate=True).astype(jnp.bfloat16)


def down_kernel(place, a0, a1, a2, a3, own, other, *rest):
    outs, (held, made) = rest[:RING], rest[RING:]
    y, z = place[1], place[2]
    for behind, block in enumerate((a0, a1, a2, a3)):
        held[lax.rem(z + RING - behind, RING)] = block[...]
    rows = held.shape[0] * held.shape[1]
    half = own.shape[2]
    act = held[...].reshape(rows, held.shape[2])
    for xl in range(2):
        for rel, part in enumerate((own, other)):
            k = (xl * 2 + rel) * half
            total = jnp.dot(act, part[xl], preferred_element_type=jnp.float32)
            made[:, :, k : k + half] = total.astype(jnp.bfloat16).reshape(
                RING, rows // RING, half
            )
    for ahead in range(RING):
        outs[ahead][...] = made[lax.rem(y + ahead, RING)]


def to_ahead(block, axis, distance):
    return lax.ppermute(block, axis, [(i, (i + distance) % RING) for i in range(RING)])


def send_each(blocks, axis):
    moved = {d: to_ahead(blocks[d], axis, d) for d in (2, 1, 3)}
    return [blocks[0], moved[1], moved[2], moved[3]]


def gather_behind(block, axis):
    return send_each([block] * RING, axis)


def swap_core(block):
    return lax.ppermute(block, "core", [(0, 1), (1, 0)])


def grid_move(block, target):
    route = [
        (y * RING + z, target(y, z)[0] * RING + target(y, z)[1])
        for y in range(RING)
        for z in range(RING)
    ]
    return lax.ppermute(block, ("y", "z"), route)


def per_device(patches, field_mask, order, embed_weight, embed_bias, norm_gain, w_up, w_down):
    xh, core, y, xl, z = (lax.axis_index(name) for name in AXES)
    first = core == 0
    tokens = patches.shape[1]
    width = embed_weight.shape[2]
    rows_up = w_up.shape[1]
    hidden = w_up.shape[2]
    half = rows_up // 2
    narrow = width // RING
    place = jnp.stack([core, y, z]).astype(jnp.int32)

    gain = lax.dynamic_slice(norm_gain[0], ((xl * RING + z) * rows_up,), (rows_up,))
    up = (w_up[0].astype(jnp.float32) * gain[:, None]).astype(jnp.bfloat16)
    down = w_down[0]
    up_low, up_high = up[:half], up[half:]
    down_low, down_high = down[:, :half], down[:, half:]
    up_got = swap_core(jnp.where(first, up_high, up_low))
    down_got = swap_core(jnp.where(first, down_high, down_low))
    ups, downs = [], []
    for kind in range(2):
        for low, high, got, into in ((up_low, up_high, up_got, ups), (down_low, down_high, down_got, downs)):
            mine = jnp.where(first, low, got) if kind == 0 else jnp.where(first, got, high)
            own = lax.all_gather(mine, ("xh", "xl"), axis=0, tiled=False)
            into.append((own, swap_core(own)))

    chosen = order[2 * xh + core]
    piece = lax.dynamic_index_in_dim(patches, chosen, 0, keepdims=False)
    present = lax.dynamic_index_in_dim(field_mask, chosen, 0, keepdims=False)
    masked = (piece * present.astype(jnp.bfloat16)[:, :, None]).reshape(tokens, -1)
    block = jax.ShapeDtypeStruct((tokens, narrow), jnp.bfloat16)
    terms = call(
        embed_kernel,
        [block] * RING,
        [SMEM, VMEM, VMEM, VMEM, VMEM],
        flops=2 * tokens * masked.shape[1] * width,
        nbytes=2 * masked.shape[1] * width,
    )(
        place,
        masked,
        present.astype(jnp.float32),
        embed_weight.reshape(-1, width),
        embed_bias,
    )
    moved = [
        grid_move(terms[d], lambda a, b, d=d: (b, (a + d) % RING)) for d in range(RING)
    ]
    x = sum(t.astype(jnp.float32) for t in moved).astype(jnp.bfloat16)

    sent = jax.ShapeDtypeStruct((tokens, hidden + 128), jnp.bfloat16)
    acted = jax.ShapeDtypeStruct((tokens, hidden), jnp.bfloat16)
    product = 2 * RING * tokens * narrow * hidden
    for layer in range(4):
        pair = layer // 2
        up_own, up_other = (w[2 * pair : 2 * pair + 2] for w in ups[layer % 2])
        down_own, down_other = (w[2 * pair : 2 * pair + 2] for w in downs[layer % 2])
        parts = call(
            up_kernel,
            [sent] * RING,
            [SMEM] + [VMEM] * 6,
            [
                pltpu.VMEM((RING, tokens, narrow), jnp.bfloat16),
                pltpu.VMEM((RING, tokens, hidden + 128), jnp.bfloat16),
            ],
            flops=product,
            nbytes=2 * narrow * hidden,
        )(place, *gather_behind(x, "y"), up_own, up_other)
        act = call(
            lambda *refs: act_kernel(width, *refs), acted, [VMEM] * RING, nbytes=8 * tokens * hidden
        )(*send_each(parts, "z"))
        parts = call(
            down_kernel,
            [block] * RING,
            [SMEM] + [VMEM] * 6,
            [
                pltpu.VMEM((RING, tokens, hidden), jnp.bfloat16),
                pltpu.VMEM((RING, tokens, narrow), jnp.bfloat16),
            ],
            flops=product,
            nbytes=2 * narrow * hidden,
        )(place, *gather_behind(act, "z"), down_own, down_other)
        total = sum(t.astype(jnp.float32) for t in send_each(parts, "y"))
        x = (x.astype(jnp.float32) + total).astype(jnp.bfloat16)

    quarters = x.reshape(tokens, 2, 2, half)
    quarters = jnp.where(first, quarters, quarters[:, :, ::-1])
    low, high = (quarters[:, i].reshape(tokens, 2 * half) for i in range(2))
    even = z % 2 == 0
    one = grid_move(
        jnp.where(even, low, high), lambda a, b: (b // 2 if b % 2 == 0 else 2 + b // 2, a)
    )
    two = grid_move(
        jnp.where(even, high, low), lambda a, b: (2 + b // 2 if b % 2 == 0 else b // 2, a)
    )
    front = y < 2
    out = jnp.concatenate([jnp.where(front, one, two), jnp.where(front, two, one)], axis=1)
    return out[None]


def solution(mesh):
    inner = Mesh(mesh.devices.reshape(SIZES), AXES)
    section, field, dp = ("xh", "core"), "y", ("xl", "z")
    in_specs = (
        P(None, dp, field, None),
        P(None, dp, field),
        P(),
        P(field, None, None),
        P(field, None),
        P(section, None),
        P(section, dp, field),
        P(section, field, dp),
    )
    return jax.shard_map(
        per_device, mesh=inner, in_specs=in_specs, out_specs=P(section, dp, field), check_vma=False
    )
```

time: 878 us -> 479 us (0.55)
  waiting for transfers between devices: 735 us -> 316 us
  starting transfers between devices: 9.12 us -> 84.5 us
  matrix products: 66.8 us -> 0 us
  Pallas kernels: 0 us -> 27.1 us
  other arithmetic: 21.3 us -> 6.83 us
    all_gather x9 -> x4, waiting for transfers between devices: 439 us -> 73.1 us  [per_device(): own = lax.all_gather(mine, ('xh', 'xl'), axis=0, tiled=False)]
    reduce_scatter x12 -> x0, waiting for transfers between devices: 291 us -> none  [the longest x7 165 us: per_device(): lax.psum_scatter(run_part.astype(jnp.bfloat16), 'field', scatter_dimensio...]
    ppermute x6 -> x60, waiting for transfers between devices: 3.39 us -> 242 us  [the longest x48 200 us: to_ahead(): lax.ppermute(block, axis, [(i, (i + distance) % RING) for i in range(RING)])]
    ppermute x6 -> x60, starting transfers between devices: 7.83 us -> 84.4 us  [the longest x48 66.4 us: to_ahead(): lax.ppermute(block, axis, [(i, (i + distance) % RING) for i in range(RING)])]
    dot_general x12 -> x0, matrix products: 66.8 us -> none  [the longest x4 46.1 us: local_layer(): part = jnp.dot(active, down_full, preferred_element_type=jnp.float32)]
    pallas_call x0 -> x13, Pallas kernels: none -> 27.1 us  [the longest x4 11.9 us: per_device(): call(up_kernel, [sent] * RING, [SMEM] + [VMEM] * 6, [pltpu.VMEM((RING, to...]
    slice x3 -> x8, local copies, waits for them, and re-layouts: 1.85 us -> 11 us  [the longest x4 7.36 us: per_device(): up_own, up_other = (w[2 * pair:2 * pair + 2] for w in ups[layer % 2])]
  transfers between devices with their start and end apart: 27 -> 64, of which waited for: 24 -> 48; matrix products, arithmetic and copies ran while one was open for 2% -> 3% of each run, Pallas kernels for 0% -> 3%
where the time goes in v1:
time: 479 us; the launch traced here: 470 us
  waiting for transfers between devices  316 us (66%)
  starting transfers between devices  84.5 us (18%)
  Pallas kernels  27.1 us (6%)
  local copies, waits for them, and re-layouts  20.3 us (4%)
  between operations  15.6 us (3%)
  other arithmetic  6.83 us (1%)
    ppermute x48, waiting for transfers between devices, to_ahead(): lax.ppermute(block, axis, [(i, (i + distance) % RING) for i in range(RING)])  200 us
    all_gather x4, waiting for transfers between devices, per_device(): own = lax.all_gather(mine, ('xh', 'xl'), axis=0, tiled=False)  73.1 us
    ppermute x48, starting transfers between devices, to_ahead(): lax.ppermute(block, axis, [(i, (i + distance) % RING) for i in range(RING)])  66.4 us
    ppermute x6, waiting for transfers between devices, grid_move(): return lax.ppermute(block, ('y', 'z'), route)  37.5 us
    ppermute x6, starting transfers between devices, grid_move(): return lax.ppermute(block, ('y', 'z'), route)  17.6 us
    pallas_call x4, Pallas kernels, per_device(): call(up_kernel, [sent] * RING, [SMEM] + [VMEM] * 6, [pltpu.VMEM((RING, to...  11.9 us
    pallas_call x4, Pallas kernels, per_device(): call(down_kernel, [block] * RING, [SMEM] + [VMEM] * 6, [pltpu.VMEM((RING,...  9.75 us
  transfers between devices with their start and end apart: 64, of which 48 were waited for; matrix products, arithmetic and copies ran while one was open for 3% of the time, Pallas kernels for 3%

profile of v1, /device:TPU:24, one launch (start us, length us, event | category | flops | bytes accessed | tf_op | source)
XLA Modules:
  0.0 470.0 jit_solution(8001581351837665989)
XLA Ops:
  17.2 35.1 %all-gather.9.cloned.1.call-done = bf16[1024,1408]{1,0:T(8,128)(2,1)} async-done(((bf16[256,1408]{1,0:T(8,128)(2,1)}), bf16[1024,1408]{1,0:T(8,128)(2,1)}) %all-gather.9.cloned.1.call-update) | async-done | bytes 2883600 | tf_op jit(solution)/shard_map/all_gather | solution.py:160
  66.4 25.1 %all-gather.11.cloned.1.call-done = bf16[5632,256]{1,0:T(8,128)(2,1)} async-done(((bf16[1408,256]{1,0:T(8,128)(2,1)}), bf16[5632,256]{1,0:T(8,128)(2,1)}) %all-gather.11.cloned.1.call-update) | async-done | bytes 2883600 | tf_op jit(solution)/shard_map/all_gather | solution.py:160
  98.8 16.6 %collective-permute-done.1 = bf16[128,1024]{1,0:T(8,128)(2,1)S(1)} collective-permute-done((bf16[128,1024]{1,0:T(8,128)(2,1)S(1)}, bf16[128,1024]{1,0:T(8,128)(2,1)S(1)}, u32[]{:S(2)}, u32[]{:S(2)}) %collective-permute-start.1) | collective-permute-done | bytes 262176 | tf_op jit(solution)/shard_map/ppermute | solution.py:135
  126.5 7.5 %collective-permute-start.5 = (bf16[128,1024]{1,0:T(8,128)(2,1)S(1)}, bf16[128,1024]{1,0:T(8,128)(2,1)}, u32[]{:S(2)}, u32[]{:S(2)}) collective-permute-start(bf16[128,1024]{1,0:T(8,128)(2,1)S(1)} %add_convert_fusion.4.x0), channel_id=1, source_target_pairs={{0,16},{8,24},{16,0},{24,8},{1,17},{9,25},{17,1},{25,9},{2,18},{10... | collective-permute-start | bytes 786440 | tf_op jit(solution)/shard_map/ppermute | solution.py:113
  156.8 12.9 %all-gather.15.cloned.1.call-done = bf16[5632,256]{1,0:T(8,128)(2,1)} async-done(((bf16[1408,256]{1,0:T(8,128)(2,1)}), bf16[5632,256]{1,0:T(8,128)(2,1)}) %all-gather.15.cloned.1.call-update) | async-done | bytes 2883600 | tf_op jit(solution)/shard_map/all_gather | solution.py:160
  185.7 8.5 %collective-permute-done.13.a2 = bf16[128,1408]{1,0:T(8,128)(2,1)S(1)} collective-permute-done((bf16[128,1408]{1,0:T(8,128)(2,1)S(1)}, bf16[128,1408]{1,0:T(8,128)(2,1)S(1)}, u32[]{:S(2)}, u32[]{:S(2)}) %collective-permute-start.13) | collective-permute-done | bytes 360480 | tf_op jit(solution)/shard_map/ppermute | solution.py:113
  199.2 6.7 %collective-permute-done.17 = bf16[128,1024]{1,0:T(8,128)(2,1)S(1)} collective-permute-done((bf16[128,1024]{1,0:T(8,128)(2,1)S(1)}, bf16[128,1024]{1,0:T(8,128)(2,1)S(1)}, u32[]{:S(2)}, u32[]{:S(2)}) %collective-permute-start.17) | collective-permute-done | bytes 262176 | tf_op jit(solution)/shard_map/ppermute | solution.py:113
  234.8 7.3 %collective-permute-done.24.refs_1_ = bf16[128,1536]{1,0:T(8,128)(2,1)S(1)} collective-permute-done((bf16[128,1536]{1,0:T(8,128)(2,1)S(1)}, bf16[128,1536]{1,0:T(8,128)(2,1)S(1)}, u32[]{:S(2)}, u32[]{:S(2)}) %collective-permute-start.24) | collective-permute-done | bytes 393248 | tf_op jit(solution)/shard_map/ppermute | solution.py:113
  242.1 9.6 %collective-permute-done.25.refs_2_ = bf16[128,1536]{1,0:T(8,128)(2,1)S(1)} collective-permute-done((bf16[128,1536]{1,0:T(8,128)(2,1)S(1)}, bf16[128,1536]{1,0:T(8,128)(2,1)S(1)}, u32[]{:S(2)}, u32[]{:S(2)}) %collective-permute-start.25) | collective-permute-done | bytes 393248 | tf_op jit(solution)/shard_map/ppermute | solution.py:113
  263.0 8.9 %collective-permute-done.28.a2 = bf16[128,1408]{1,0:T(8,128)(2,1)S(1)} collective-permute-done((bf16[128,1408]{1,0:T(8,128)(2,1)S(1)}, bf16[128,1408]{1,0:T(8,128)(2,1)S(1)}, u32[]{:S(2)}, u32[]{:S(2)}) %collective-permute-start.28) | collective-permute-done | bytes 360480 | tf_op jit(solution)/shard_map/ppermute | solution.py:113
  277.2 6.4 %collective-permute-done.31 = bf16[128,1024]{1,0:T(8,128)(2,1)S(1)} collective-permute-done((bf16[128,1024]{1,0:T(8,128)(2,1)S(1)}, bf16[128,1024]{1,0:T(8,128)(2,1)S(1)}, u32[]{:S(2)}, u32[]{:S(2)}) %collective-permute-start.31) | collective-permute-done | bytes 262176 | tf_op jit(solution)/shard_map/ppermute | solution.py:113
  292.3 6.2 %collective-permute-done.34.x1 = bf16[128,1024]{1,0:T(8,128)(2,1)S(1)} collective-permute-done((bf16[128,1024]{1,0:T(8,128)(2,1)S(1)}, bf16[128,1024]{1,0:T(8,128)(2,1)S(1)}, u32[]{:S(2)}, u32[]{:S(2)}) %collective-permute-start.34) | collective-permute-done | bytes 262176 | tf_op jit(solution)/shard_map/ppermute | solution.py:113
  312.2 7.5 %collective-permute-done.37.refs_1_ = bf16[128,1536]{1,0:T(8,128)(2,1)S(1)} collective-permute-done((bf16[128,1536]{1,0:T(8,128)(2,1)S(1)}, bf16[128,1536]{1,0:T(8,128)(2,1)S(1)}, u32[]{:S(2)}, u32[]{:S(2)}) %collective-permute-start.37) | collective-permute-done | bytes 393248 | tf_op jit(solution)/shard_map/ppermute | solution.py:113
  319.7 9.6 %collective-permute-done.38.refs_2_ = bf16[128,1536]{1,0:T(8,128)(2,1)S(1)} collective-permute-done((bf16[128,1536]{1,0:T(8,128)(2,1)S(1)}, bf16[128,1536]{1,0:T(8,128)(2,1)S(1)}, u32[]{:S(2)}, u32[]{:S(2)}) %collective-permute-start.38) | collective-permute-done | bytes 393248 | tf_op jit(solution)/shard_map/ppermute | solution.py:113
  334.4 6.3 %collective-permute-done.40.a1 = bf16[128,1408]{1,0:T(8,128)(2,1)S(1)} collective-permute-done((bf16[128,1408]{1,0:T(8,128)(2,1)S(1)}, bf16[128,1408]{1,0:T(8,128)(2,1)S(1)}, u32[]{:S(2)}, u32[]{:S(2)}) %collective-permute-start.40) | collective-permute-done | bytes 360480 | tf_op jit(solution)/shard_map/ppermute | solution.py:113
  340.6 8.9 %collective-permute-done.41.a2 = bf16[128,1408]{1,0:T(8,128)(2,1)S(1)} collective-permute-done((bf16[128,1408]{1,0:T(8,128)(2,1)S(1)}, bf16[128,1408]{1,0:T(8,128)(2,1)S(1)}, u32[]{:S(2)}, u32[]{:S(2)}) %collective-permute-start.41) | collective-permute-done | bytes 360480 | tf_op jit(solution)/shard_map/ppermute | solution.py:113
  354.8 6.5 %collective-permute-done.43 = bf16[128,1024]{1,0:T(8,128)(2,1)S(1)} collective-permute-done((bf16[128,1024]{1,0:T(8,128)(2,1)S(1)}, bf16[128,1024]{1,0:T(8,128)(2,1)S(1)}, u32[]{:S(2)}, u32[]{:S(2)}) %collective-permute-start.43) | collective-permute-done | bytes 262176 | tf_op jit(solution)/shard_map/ppermute | solution.py:113
  369.7 6.4 %collective-permute-done.46.x1 = bf16[128,1024]{1,0:T(8,128)(2,1)S(1)} collective-permute-done((bf16[128,1024]{1,0:T(8,128)(2,1)S(1)}, bf16[128,1024]{1,0:T(8,128)(2,1)S(1)}, u32[]{:S(2)}, u32[]{:S(2)}) %collective-permute-start.46) | collective-permute-done | bytes 262176 | tf_op jit(solution)/shard_map/ppermute | solution.py:113
  389.8 7.5 %collective-permute-done.49.refs_1_ = bf16[128,1536]{1,0:T(8,128)(2,1)S(1)} collective-permute-done((bf16[128,1536]{1,0:T(8,128)(2,1)S(1)}, bf16[128,1536]{1,0:T(8,128)(2,1)S(1)}, u32[]{:S(2)}, u32[]{:S(2)}) %collective-permute-start.49) | collective-permute-done | bytes 393248 | tf_op jit(solution)/shard_map/ppermute | solution.py:113
  397.3 9.6 %collective-permute-done.50.refs_2_ = bf16[128,1536]{1,0:T(8,128)(2,1)S(1)} collective-permute-done((bf16[128,1536]{1,0:T(8,128)(2,1)S(1)}, bf16[128,1536]{1,0:T(8,128)(2,1)S(1)}, u32[]{:S(2)}, u32[]{:S(2)}) %collective-permute-start.50) | collective-permute-done | bytes 393248 | tf_op jit(solution)/shard_map/ppermute | solution.py:113
  412.2 6.1 %collective-permute-done.52.a1 = bf16[128,1408]{1,0:T(8,128)(2,1)S(1)} collective-permute-done((bf16[128,1408]{1,0:T(8,128)(2,1)S(1)}, bf16[128,1408]{1,0:T(8,128)(2,1)S(1)}, u32[]{:S(2)}, u32[]{:S(2)}) %collective-permute-start.52) | collective-permute-done | bytes 360480 | tf_op jit(solution)/shard_map/ppermute | solution.py:113
  418.3 8.9 %collective-permute-done.53.a2 = bf16[128,1408]{1,0:T(8,128)(2,1)S(1)} collective-permute-done((bf16[128,1408]{1,0:T(8,128)(2,1)S(1)}, bf16[128,1408]{1,0:T(8,128)(2,1)S(1)}, u32[]{:S(2)}, u32[]{:S(2)}) %collective-permute-start.53) | collective-permute-done | bytes 360480 | tf_op jit(solution)/shard_map/ppermute | solution.py:113
  432.5 6.5 %collective-permute-done.55 = bf16[128,1024]{1,0:T(8,128)(2,1)S(1)} collective-permute-done((bf16[128,1024]{1,0:T(8,128)(2,1)S(1)}, bf16[128,1024]{1,0:T(8,128)(2,1)S(1)}, u32[]{:S(2)}, u32[]{:S(2)}) %collective-permute-start.55) | collective-permute-done | bytes 262176 | tf_op jit(solution)/shard_map/ppermute | solution.py:113
  452.2 8.6 %collective-permute-done.58 = bf16[128,512]{1,0:T(8,128)(2,1)S(1)} collective-permute-done((bf16[128,512]{1,0:T(8,128)(2,1)S(1)}, bf16[128,512]{1,0:T(8,128)(2,1)S(1)}, u32[]{:S(2)}, u32[]{:S(2)}) %collective-permute-start.58) | collective-permute-done | bytes 131104 | tf_op jit(solution)/shard_map/ppermute | solution.py:135
  (184 shorter events, 211.4 us)
Async XLA Ops:
  6.5 45.7 %all-gather.9.cloned.1.call-start = ((), (), s32[]{:S(2)}) async-start(), calls=%async_computation | async-start | bytes 3604480 | tf_op jit(solution)/shard_map/all_gather | solution.py:160
  12.7 78.8 %all-gather.11.cloned.1.call-start = ((), (), s32[]{:S(2)}) async-start(), calls=%async_computation.1 | async-start | bytes 3604480 | tf_op jit(solution)/shard_map/all_gather | solution.py:160
  16.4 119.6 %all-gather.13.cloned.1.call-start = ((), (), s32[]{:S(2)}) async-start(), calls=%async_computation.2 | async-start | bytes 3604480 | tf_op jit(solution)/shard_map/all_gather | solution.py:160
  17.1 152.6 %all-gather.15.cloned.1.call-start = ((), (), s32[]{:S(2)}) async-start(), calls=%async_computation.3 | async-start | bytes 3604480 | tf_op jit(solution)/shard_map/all_gather | solution.py:160
  52.3 83.8 %collective-permute-start.8 = (bf16[4,256,1408]{2,1,0:T(8,128)(2,1)}, bf16[4,256,1408]{2,1,0:T(8,128)(2,1)}, u32[]{:S(2)}, u32[]{:S(2)}) collective-permute-start(bf16[4,256,1408]{2,1,0:T(8,128)(2,1)} %bitcast.53), channel_id=1, source_target_pairs={{0,32},{32,0},{1,33},{33,1},{2,34},{34,2},{3,35},{35,3},{4,36},{36... | collective-permute-start | bytes 8650760 | tf_op jit(solution)/shard_map/ppermute | solution.py:126
  61.6 32.8 %collective-permute-start = (bf16[128,1024]{1,0:T(8,128)(2,1)S(1)}, bf16[128,1024]{1,0:T(8,128)(2,1)S(1)}, u32[]{:S(2)}, u32[]{:S(2)}) collective-permute-start(bf16[128,1024]{1,0:T(8,128)(2,1)S(1)} %get-tuple-element.41), channel_id=1, source_target_pairs={{0,0},{1,8},{2,16},{3,24},{8,1},{9,9},{10,17},{11,25},{16,2},{17,1... | collective-permute-start | bytes 786440 | tf_op jit(solution)/shard_map/ppermute | solution.py:135
  91.5 86.9 %collective-permute-start.16 = (bf16[4,1408,256]{2,1,0:T(8,128)(2,1)}, bf16[4,1408,256]{2,1,0:T(8,128)(2,1)}, u32[]{:S(2)}, u32[]{:S(2)}) collective-permute-start(bf16[4,1408,256]{2,1,0:T(8,128)(2,1)} %bitcast.52), channel_id=1, source_target_pairs={{0,32},{32,0},{1,33},{33,1},{2,34},{34,2},{3,35},{35,3},{4,36},{36... | collective-permute-start | bytes 8650760 | tf_op jit(solution)/shard_map/ppermute | solution.py:126
  91.5 23.9 %collective-permute-start.1 = (bf16[128,1024]{1,0:T(8,128)(2,1)S(1)}, bf16[128,1024]{1,0:T(8,128)(2,1)S(1)}, u32[]{:S(2)}, u32[]{:S(2)}) collective-permute-start(bf16[128,1024]{1,0:T(8,128)(2,1)S(1)} %get-tuple-element.42), channel_id=1, source_target_pairs={{0,1},{1,9},{2,17},{3,25},{8,2},{9,10},{10,18},{11,26},{16,3},{17,... | collective-permute-start | bytes 786440 | tf_op jit(solution)/shard_map/ppermute | solution.py:135
  92.0 29.1 %collective-permute-start.2 = (bf16[128,1024]{1,0:T(8,128)(2,1)S(1)}, bf16[128,1024]{1,0:T(8,128)(2,1)S(1)}, u32[]{:S(2)}, u32[]{:S(2)}) collective-permute-start(bf16[128,1024]{1,0:T(8,128)(2,1)S(1)} %get-tuple-element.43), channel_id=1, source_target_pairs={{0,2},{1,10},{2,18},{3,26},{8,3},{9,11},{10,19},{11,27},{16,0},{17... | collective-permute-start | bytes 786440 | tf_op jit(solution)/shard_map/ppermute | solution.py:135
  94.4 31.8 %collective-permute-start.3 = (bf16[128,1024]{1,0:T(8,128)(2,1)S(1)}, bf16[128,1024]{1,0:T(8,128)(2,1)S(1)}, u32[]{:S(2)}, u32[]{:S(2)}) collective-permute-start(bf16[128,1024]{1,0:T(8,128)(2,1)S(1)} %get-tuple-element.44), channel_id=1, source_target_pairs={{0,3},{1,11},{2,19},{3,27},{8,0},{9,8},{10,16},{11,24},{16,1},{17,... | collective-permute-start | bytes 786440 | tf_op jit(solution)/shard_map/ppermute | solution.py:135
  136.1 78.4 %collective-permute-start.23 = (bf16[4,256,1408]{2,1,0:T(8,128)(2,1)}, bf16[4,256,1408]{2,1,0:T(8,128)(2,1)}, u32[]{:S(2)}, u32[]{:S(2)}) collective-permute-start(bf16[4,256,1408]{2,1,0:T(8,128)(2,1)} %bitcast.51), channel_id=1, source_target_pairs={{0,32},{32,0},{1,33},{33,1},{2,34},{34,2},{3,35},{35,3},{4,36},{36... | collective-permute-start | bytes 8650760 | tf_op jit(solution)/shard_map/ppermute | solution.py:126
  150.8 18.9 %collective-permute-start.10 = (bf16[128,1536]{1,0:T(8,128)(2,1)}, bf16[128,1536]{1,0:T(8,128)(2,1)}, u32[]{:S(2)}, u32[]{:S(2)}) collective-permute-start(bf16[128,1536]{1,0:T(8,128)(2,1)} %get-tuple-element.47), channel_id=1, source_target_pairs={{0,2},{1,3},{2,0},{3,1},{4,6},{5,7},{6,4},{7,5},{8,10},{9,11},{10,... | collective-permute-start | bytes 1179656 | tf_op jit(solution)/shard_map/ppermute | solution.py:113
  153.5 19.3 %collective-permute-start.11 = (bf16[128,1536]{1,0:T(8,128)(2,1)}, bf16[128,1536]{1,0:T(8,128)(2,1)}, u32[]{:S(2)}, u32[]{:S(2)}) collective-permute-start(bf16[128,1536]{1,0:T(8,128)(2,1)} %get-tuple-element.48), channel_id=1, source_target_pairs={{0,3},{1,0},{2,1},{3,2},{4,7},{5,4},{6,5},{7,6},{8,11},{9,8},{10,9... | collective-permute-start | bytes 1179656 | tf_op jit(solution)/shard_map/ppermute | solution.py:113
  154.2 18.7 %collective-permute-start.9 = (bf16[128,1536]{1,0:T(8,128)(2,1)}, bf16[128,1536]{1,0:T(8,128)(2,1)}, u32[]{:S(2)}, u32[]{:S(2)}) collective-permute-start(bf16[128,1536]{1,0:T(8,128)(2,1)} %get-tuple-element.46), channel_id=1, source_target_pairs={{0,1},{1,2},{2,3},{3,0},{4,5},{5,6},{6,7},{7,4},{8,9},{9,10},{10,1... | collective-permute-start | bytes 1179656 | tf_op jit(solution)/shard_map/ppermute | solution.py:113
  169.7 87.1 %collective-permute-start.30 = (bf16[4,1408,256]{2,1,0:T(8,128)(2,1)}, bf16[4,1408,256]{2,1,0:T(8,128)(2,1)S(1)}, u32[]{:S(2)}, u32[]{:S(2)}) collective-permute-start(bf16[4,1408,256]{2,1,0:T(8,128)(2,1)} %bitcast.50), channel_id=1, source_target_pairs={{0,32},{32,0},{1,33},{33,1},{2,34},{34,2},{3,35},{35,3},{4,36},{36... | collective-permute-start | bytes 8650760 | tf_op jit(solution)/shard_map/ppermute | solution.py:126
  175.1 19.1 %collective-permute-start.13 = (bf16[128,1408]{1,0:T(8,128)(2,1)S(1)}, bf16[128,1408]{1,0:T(8,128)(2,1)S(1)}, u32[]{:S(2)}, u32[]{:S(2)}) collective-permute-start(bf16[128,1408]{1,0:T(8,128)(2,1)S(1)} %shard_map.84.a0), channel_id=1, source_target_pairs={{0,2},{1,3},{2,0},{3,1},{4,6},{5,7},{6,4},{7,5},{8,10},{9,11},{10,... | collective-permute-start | bytes 1081352 | tf_op jit(solution)/shard_map/ppermute | solution.py:113
  231.8 19.8 %collective-permute-start.25 = (bf16[128,1536]{1,0:T(8,128)(2,1)S(1)}, bf16[128,1536]{1,0:T(8,128)(2,1)S(1)}, u32[]{:S(2)}, u32[]{:S(2)}) collective-permute-start(bf16[128,1536]{1,0:T(8,128)(2,1)S(1)} %get-tuple-element.55), channel_id=1, source_target_pairs={{0,2},{1,3},{2,0},{3,1},{4,6},{5,7},{6,4},{7,5},{8,10},{9,11},{10,... | collective-permute-start | bytes 1179656 | tf_op jit(solution)/shard_map/ppermute | solution.py:113
  253.5 18.4 %collective-permute-start.28 = (bf16[128,1408]{1,0:T(8,128)(2,1)S(1)}, bf16[128,1408]{1,0:T(8,128)(2,1)S(1)}, u32[]{:S(2)}, u32[]{:S(2)}) collective-permute-start(bf16[128,1408]{1,0:T(8,128)(2,1)S(1)} %shard_map.87.a0), channel_id=1, source_target_pairs={{0,2},{1,3},{2,0},{3,1},{4,6},{5,7},{6,4},{7,5},{8,10},{9,11},{10,... | collective-permute-start | bytes 1081352 | tf_op jit(solution)/shard_map/ppermute | solution.py:113
  309.5 19.8 %collective-permute-start.38 = (bf16[128,1536]{1,0:T(8,128)(2,1)S(1)}, bf16[128,1536]{1,0:T(8,128)(2,1)S(1)}, u32[]{:S(2)}, u32[]{:S(2)}) collective-permute-start(bf16[128,1536]{1,0:T(8,128)(2,1)S(1)} %get-tuple-element.63), channel_id=1, source_target_pairs={{0,2},{1,3},{2,0},{3,1},{4,6},{5,7},{6,4},{7,5},{8,10},{9,11},{10,... | collective-permute-start | bytes 1179656 | tf_op jit(solution)/shard_map/ppermute | solution.py:113
  311.9 17.4 %collective-permute-start.39 = (bf16[128,1536]{1,0:T(8,128)(2,1)S(1)}, bf16[128,1536]{1,0:T(8,128)(2,1)S(1)}, u32[]{:S(2)}, u32[]{:S(2)}) collective-permute-start(bf16[128,1536]{1,0:T(8,128)(2,1)S(1)} %get-tuple-element.64), channel_id=1, source_target_pairs={{0,3},{1,0},{2,1},{3,2},{4,7},{5,4},{6,5},{7,6},{8,11},{9,8},{10,9... | collective-permute-start | bytes 1179656 | tf_op jit(solution)/shard_map/ppermute | solution.py:113
  331.1 18.4 %collective-permute-start.41 = (bf16[128,1408]{1,0:T(8,128)(2,1)S(1)}, bf16[128,1408]{1,0:T(8,128)(2,1)S(1)}, u32[]{:S(2)}, u32[]{:S(2)}) collective-permute-start(bf16[128,1408]{1,0:T(8,128)(2,1)S(1)} %shard_map.90.a0), channel_id=1, source_target_pairs={{0,2},{1,3},{2,0},{3,1},{4,6},{5,7},{6,4},{7,5},{8,10},{9,11},{10,... | collective-permute-start | bytes 1081352 | tf_op jit(solution)/shard_map/ppermute | solution.py:113
  387.1 19.9 %collective-permute-start.50 = (bf16[128,1536]{1,0:T(8,128)(2,1)S(1)}, bf16[128,1536]{1,0:T(8,128)(2,1)S(1)}, u32[]{:S(2)}, u32[]{:S(2)}) collective-permute-start(bf16[128,1536]{1,0:T(8,128)(2,1)S(1)} %get-tuple-element.71), channel_id=1, source_target_pairs={{0,2},{1,3},{2,0},{3,1},{4,6},{5,7},{6,4},{7,5},{8,10},{9,11},{10,... | collective-permute-start | bytes 1179656 | tf_op jit(solution)/shard_map/ppermute | solution.py:113
  389.5 17.4 %collective-permute-start.51 = (bf16[128,1536]{1,0:T(8,128)(2,1)S(1)}, bf16[128,1536]{1,0:T(8,128)(2,1)S(1)}, u32[]{:S(2)}, u32[]{:S(2)}) collective-permute-start(bf16[128,1536]{1,0:T(8,128)(2,1)S(1)} %get-tuple-element.72), channel_id=1, source_target_pairs={{0,3},{1,0},{2,1},{3,2},{4,7},{5,4},{6,5},{7,6},{8,11},{9,8},{10,9... | collective-permute-start | bytes 1179656 | tf_op jit(solution)/shard_map/ppermute | solution.py:113
  408.7 18.5 %collective-permute-start.53 = (bf16[128,1408]{1,0:T(8,128)(2,1)S(1)}, bf16[128,1408]{1,0:T(8,128)(2,1)S(1)}, u32[]{:S(2)}, u32[]{:S(2)}) collective-permute-start(bf16[128,1408]{1,0:T(8,128)(2,1)S(1)} %shard_map.93.a0), channel_id=1, source_target_pairs={{0,2},{1,3},{2,0},{3,1},{4,6},{5,7},{6,4},{7,5},{8,10},{9,11},{10,... | collective-permute-start | bytes 1081352 | tf_op jit(solution)/shard_map/ppermute | solution.py:113
  (53 other events, 647.3 us)
Sparse Core Ops, SparseCore 0:
  12.8 39.4 all-gather.8
  53.9 37.5 all-gather.10
  93.2 37.4 all-gather.12
  132.2 37.4 all-gather.14
